TPU v7x, 128 devices: a whole 4x4x4 slice. The times are simulated.
128 devices in a mesh: wide: 16 (over z, x), narrow: 8 (over y, core).
Axes of the slice: x: 4, y: 4, z: 4, core: 2. Of those that a mesh axis runs over, the one named last changes fastest.
Arguments:
- cotangent: float32 [1536, 256, 256], P(('wide', 'narrow')), may hold values from -6 to 6
- row_basis: float32 [1536, 256, 128], P(('wide', 'narrow')), may hold values from -0.375 to 0.375
- col_basis: float32 [1536, 256, 128], P(('wide', 'narrow')), may hold values from -0.5 to 0.5
- leaf_up: float32 [1536, 128, 128], P(('wide', 'narrow')), may hold values from -0.15625 to 0.15625
- node_up: float32 [128, 128, 128], P(('wide', 'narrow')), may hold values from -0.1875 to 0.1875
- node_couple: float32 [128, 2, 128, 128], P(('wide', 'narrow')), may hold values from -0.375 to 0.375
- group_couple: float32 [16, 8, 128, 128], P('wide', 'narrow'), may hold values from -0.1875 to 0.1875
- node_down: float32 [128, 128, 128], P(('wide', 'narrow')), may hold values from -0.5 to 0.5
- leaf_down: float32 [1536, 128, 128], P(('wide', 'narrow')), may hold values from -0.5 to 0.5
- near_blocks: float32 [1536, 4, 256, 256], P(('wide', 'narrow')), may hold values from -0.1875 to 0.1875
- near_index: int32 [1536, 4], P(('wide', 'narrow')), may hold values from 0 to 1535, as said below
- far_nodes: int32 [128, 2], P(('wide', 'narrow')), may hold values from 0 to 7, as said below
- far_groups: int32 [16, 8], P('wide', 'narrow'), may hold values from 0 to 15, as said below
Outputs:
- product: float32 [1536, 256, 256], P(('wide', 'narrow'))
Inputs may be any that keep to these rules, and one draw needn't show every extreme that they name: near_index[l, 0] is l; every other entry differs from l by 1 to 2. far_nodes[d, j] never equals d % 8; the entries of a row differ. far_groups[g, j] never equals g; the entries of a row differ.
All inputs are finite; a program needn't handle non-finite values.
Results may differ from a plain program's by a relative error of at most 0.000062.
Values sent between devices are 32-bit elements; how exact they have to be, the bound alone decides.
A program may use at most 128 MiB of HBM per device.

v0:
```python
import jax
import jax.numpy as jnp
from jax import lax
from jax.sharding import PartitionSpec as P

NEAR_REACH = 2
HIGH = lax.Precision.HIGHEST


def from_behind(value, axis, steps):
    count = lax.axis_size(axis)
    leading, last = (max(0, -steps), min(count, count - steps))
    return lax.ppermute(value, axis, [(source, source + steps) for source in range(leading, last)])


def shards(
    cotangent,
    row_basis,
    col_basis,
    leaf_up,
    node_up,
    node_couple,
    group_couple,
    node_down,
    leaf_down,
    near_blocks,
    near_index,
    far_nodes,
    far_groups,
):
    leaves = cotangent.shape[0]
    lower = from_behind(cotangent[leaves - NEAR_REACH :], ("wide", "narrow"), 1)
    upper = from_behind(cotangent[:NEAR_REACH], ("wide", "narrow"), -1)
    leaf_coeffs = jnp.einsum("lpk,lpv->lkv", row_basis, cotangent, precision=HIGH)
    node_coeffs = jnp.einsum("lkm,lkv->mv", leaf_up, leaf_coeffs, precision=HIGH)
    up_term = jnp.dot(node_up[0].T, node_coeffs, precision=HIGH)
    siblings = lax.all_gather(node_coeffs[None], "narrow", axis=0, tiled=True)
    group_coeffs = lax.psum(up_term, "narrow")
    picked = siblings[far_nodes[0]]
    node_out = jnp.einsum("jkm,jkv->mv", node_couple[0], picked, precision=HIGH)
    all_groups = lax.all_gather(group_coeffs[None], "wide", axis=0, tiled=True)
    picked_groups = all_groups[far_groups[0]]
    partial_value = jnp.einsum("jkm,jkv->mv", group_couple[0], picked_groups, precision=HIGH)
    group_out = lax.psum(partial_value, "narrow")
    node_total = node_out + jnp.dot(node_down[0], group_out, precision=HIGH)
    leaf_total = jnp.einsum("lmk,kv->lmv", leaf_down, node_total, precision=HIGH)
    far_part = jnp.einsum("lpk,lkv->lpv", col_basis, leaf_total, precision=HIGH)
    extended = jnp.concatenate([lower, cotangent, upper], axis=0)
    node_rank = lax.axis_index("wide") * lax.axis_size("narrow") + lax.axis_index("narrow")
    first_leaf = node_rank * leaves - NEAR_REACH
    local_index = near_index - first_leaf
    sources = extended[local_index]
    near_part = jnp.einsum("ljpq,ljpv->lqv", near_blocks, sources, precision=HIGH)
    return far_part + near_part


def solution(mesh):
    in_specs = (
        P(("wide", "narrow"), None, None),
        P(("wide", "narrow"), None, None),
        P(("wide", "narrow"), None, None),
        P(("wide", "narrow"), None, None),
        P(("wide", "narrow"), None, None),
        P(("wide", "narrow"), None, None, None),
        P("wide", "narrow", None, None),
        P(("wide", "narrow"), None, None),
        P(("wide", "narrow"), None, None),
        P(("wide", "narrow"), None, None, None),
        P(("wide", "narrow"), None),
        P(("wide", "narrow"), None),
        P("wide", "narrow"),
    )
    out_specs = P(("wide", "narrow"), None, None)
    return jax.shard_map(shards, mesh=mesh, in_specs=in_specs, out_specs=out_specs, check_vma=False)
```

profile of v0, /device:TPU:0, one launch (start us, length us, event | category | flops | bytes accessed | tf_op | source)
XLA Modules:
  0.0 259.9 jit_solution(13110974289088481287)
XLA Ops:
  6.5 7.7 %fusion.14 = f32[12,128,256]{1,2,0:T(8,128)S(1)} fusion(f32[12,256,128]{2,1,0:T(8,128)} %param.14, f32[12,256,256]{2,1,0:T(8,128)} %param.13), kind=kOutput, calls=%fused_computation.26 | convolution fusion | flops 1207959552 | bytes 6291456 | tf_op jit(solution)/shard_map/lpk,lpv->lkv/dot_general | solution.py:34
  14.3 1.4 fusion.15
  15.7 0.9 convolution_bitcast_fusion.2
  16.7 0.7 all-gather.6.cloned.1.call-update
  17.5 61.0 %all-reduce.3.cloned.1.call-done = f32[1,128,256]{1,2,0:T(8,128)} async-done(((f32[1,128,256]{1,2,0:T(8,128)}), f32[1,128,256]{1,2,0:T(8,128)}) %all-reduce.3.cloned.1.call-update) | async-done | bytes 131088 | tf_op jit(solution)/shard_map/psum | solution.py:38
  78.5 1.7 copy.25
  80.2 2.1 fusion.13
  82.3 1.3 collective-permute-start
  83.7 1.5 collective-permute-start.1
  86.1 1.4 collective-permute-done.1
  87.5 4.3 %pad_maximum_fusion = f32[16,256,256]{2,1,0:T(8,128)} fusion(f32[2,256,256]{2,1,0:T(8,128)S(1)} %collective-permute-done.1, f32[12,256,256]{2,1,0:T(8,128)} %param.13, f32[2,256,256]{2,1,0:T(8,128)S(1)} %collective-permute-done), kind=kLoop, calls=%fused_computation.2 | loop fusion | flops 2097152 | bytes 8388608 | tf_op jit(solution)/shard_map/concatenate | solution.py:48
  91.7 10.0 %gather_fusion.1 = f32[48,256,256]{2,1,0:T(8,128)} fusion(f32[16,256,256]{2,1,0:T(8,128)} %pad_maximum_fusion, s32[1024]{0:T(1024)S(1)} %pad_clamp_fusion), kind=kCustom, calls=%fused_computation.1 | custom fusion | bytes 25166016 | tf_op jit(solution)/shard_map/gather | solution.py:52
  101.8 5.8 %all-gather.6.cloned.1.call-done = f32[1024,256]{0,1:T(8,128)} async-done(((f32[128,256]{0,1:T(8,128)}), f32[1024,256]{0,1:T(8,128)}) %all-gather.6.cloned.1.call-update) | async-done | bytes 1048592 | tf_op jit(solution)/shard_map/all_gather | solution.py:37
  107.6 1.6 copy.34
  109.2 0.6 gather_fusion
  109.7 45.5 %all-gather.4.cloned.1.call-done = f32[16,128,256]{2,1,0:T(8,128)} async-done(((f32[1,128,256]{2,1,0:T(8,128)}), f32[16,128,256]{2,1,0:T(8,128)}) %all-gather.4.cloned.1.call-update) | async-done | bytes 2097168 | tf_op jit(solution)/shard_map/all_gather | solution.py:41
  155.2 1.9 convolution_bitcast_fusion.1
  157.2 0.6 convolution_bitcast_fusion
  157.8 58.3 %all-reduce.5.cloned.1.call-done = f32[128,256]{0,1:T(8,128)} async-done(((f32[128,256]{0,1:T(8,128)}), f32[128,256]{0,1:T(8,128)}) %all-reduce.5.cloned.1.call-update) | async-done | bytes 131088 | tf_op jit(solution)/shard_map/psum | solution.py:44
  216.1 1.2 fusion.3
  217.3 2.5 fusion.16
  219.9 2.9 %fusion.1 = f32[12,256,256]{2,1,0:T(8,128)S(1)} fusion(f32[12,256,128]{2,1,0:T(8,128)S(1)} %copy-done, f32[256,12,128]{2,0,1:T(8,128)S(1)} %fusion.16), kind=kOutput, calls=%fused_computation.5 | convolution fusion | flops 1207959552 | bytes 6291456 | tf_op jit(solution)/shard_map/lpk,lkv->lpv/dot_general | solution.py:47
  222.8 27.0 %fusion = f32[12,256,256]{1,2,0:T(8,128)} fusion(f32[12,256,256]{2,1,0:T(8,128)S(1)} %fusion.1, f32[12,4,256,256]{3,2,1,0:T(8,128)} %bitcast.62, f32[12,4,256,256]{3,2,1,0:T(8,128)} %param.22), kind=kOutput, calls=%fused_computation.4 | convolution fusion | flops 9664462848 | bytes 31457280 | tf_op jit(solution)/shard_map/ljpq,ljpv->lqv/dot_general | solution.py:53
  249.8 3.5 %copy.28 = f32[12,256,256]{2,1,0:T(8,128)} copy(f32[12,256,256]{1,2,0:T(8,128)} %fusion) | data formatting | bytes 6291456 | tf_op jit(solution)/shard_map/add | solution.py:54
  (32 shorter events, 0.4 us)
Async XLA Ops:
  6.5 213.3 %copy-start = (f32[12,256,128]{2,1,0:T(8,128)S(1)}, f32[12,256,128]{2,1,0:T(8,128)}, u32[]{:S(2)}) copy-start(f32[12,256,128]{2,1,0:T(8,128)} %param.15) | copy-start | bytes 4718596
  6.5 7.7 %copy-start.2 = (f32[12,128,128]{2,1,0:T(8,128)S(1)}, f32[12,128,128]{2,1,0:T(8,128)}, u32[]{:S(2)}) copy-start(f32[12,128,128]{2,1,0:T(8,128)} %param.16) | copy-start | bytes 2359300
  6.5 9.2 %copy-start.4 = (f32[1,128,128]{2,1,0:T(8,128)S(1)}, f32[1,128,128]{2,1,0:T(8,128)}, u32[]{:S(2)}) copy-start(f32[1,128,128]{2,1,0:T(8,128)} %param.17) | copy-start | bytes 196612
  6.5 72.0 %all-reduce.3.cloned.1.call-start = ((), (), s32[]{:S(2)}) async-start(), calls=%async_computation | async-start | bytes 262144 | tf_op jit(solution)/shard_map/psum | solution.py:38
  14.3 70.9 %copy-start.7 = (s32[12,4]{0,1:T(4,128)S(1)}, s32[12,4]{0,1:T(4,128)}, u32[]{:S(2)}) copy-start(s32[12,4]{0,1:T(4,128)} %param.23) | copy-start | bytes 580
  14.3 71.7 %copy-start.8 = (s32[1,2]{1,0:T(1,128)S(1)}, s32[1,2]{1,0:T(1,128)}, u32[]{:S(2)}) copy-start(s32[1,2]{1,0:T(1,128)} %param.24) | copy-start | bytes 28
  15.7 1.0 copy-start.1
  16.7 90.9 %all-gather.6.cloned.1.call-start = ((), (), s32[]{:S(2)}) async-start(), calls=%async_computation.3 | async-start | bytes 1179648 | tf_op jit(solution)/shard_map/all_gather | solution.py:37
  17.4 137.8 %all-gather.4.cloned.1.call-start = ((), (), s32[]{:S(2)}) async-start(), calls=%async_computation.1 | async-start | bytes 2228224 | tf_op jit(solution)/shard_map/all_gather | solution.py:41
  80.2 135.9 %all-reduce.5.cloned.1.call-start = ((), (), s32[]{:S(2)}) async-start(), calls=%async_computation.2 | async-start | bytes 262144 | tf_op jit(solution)/shard_map/psum | solution.py:44
  82.3 3.7 %collective-permute-start = (f32[2,256,256]{2,1,0:T(8,128)}, f32[2,256,256]{2,1,0:T(8,128)S(1)}, u32[]{:S(2)}, u32[]{:S(2)}) collective-permute-start(f32[2,256,256]{2,1,0:T(8,128)} %get-tuple-element.16), channel_id=1, source_target_pairs={{0,1},{1,2},{2,3},{3,4},{4,5},{5,6},{6,7},{7,8},{8,9},{9,10},{10,1... | collective-permute-start | bytes 1572872 | tf_op jit(solution)/shard_map/ppermute | solution.py:13
  83.7 3.8 %collective-permute-start.1 = (f32[2,256,256]{2,1,0:T(8,128)S(1)}, f32[2,256,256]{2,1,0:T(8,128)S(1)}, u32[]{:S(2)}, u32[]{:S(2)}) collective-permute-start(f32[2,256,256]{2,1,0:T(8,128)S(1)} %get-tuple-element.17), channel_id=1, source_target_pairs={{1,0},{2,1},{3,2},{4,3},{5,4},{6,5},{7,6},{8,7},{9,8},{10,9},{11,1... | collective-permute-start | bytes 1572872 | tf_op jit(solution)/shard_map/ppermute | solution.py:13
  91.7 63.5 %copy-start.5 = (f32[1,1,128,128]{3,2,1,0:T(8,128)S(1)}, f32[1,1,128,128]{3,2,1,0:T(8,128)}, u32[]{:S(2)}) copy-start(f32[1,1,128,128]{3,2,1,0:T(8,128)} %param.19) | copy-start | bytes 196612
  101.8 55.5 %copy-start.3 = (f32[1,2,128,128]{3,2,1,0:T(8,128)S(1)}, f32[1,2,128,128]{3,2,1,0:T(8,128)}, u32[]{:S(2)}) copy-start(f32[1,2,128,128]{3,2,1,0:T(8,128)} %param.18) | copy-start | bytes 393220
  101.8 114.4 %copy-start.6 = (f32[1,128,128]{2,1,0:T(8,128)S(1)}, f32[1,128,128]{2,1,0:T(8,128)}, u32[]{:S(2)}) copy-start(f32[1,128,128]{2,1,0:T(8,128)} %param.20) | copy-start | bytes 196612
Sparse Core Ops, SparseCore 0:
  16.8 61.6 all-reduce.2
  80.3 27.2 all-gather.5
  110.0 45.2 all-gather.3
  157.5 58.5 all-reduce.4
where the time goes:
time: 260 us
  waiting for transfers between devices  173 us (67%)
  matrix products  46.2 us (18%)
  local copies, waits for them, and re-layouts  19.7 us (8%)
  between operations  14 us (5%)
  other arithmetic  4.28 us (2%)
  starting transfers between devices  2.91 us (1%)
    psum x1, waiting for transfers between devices, shards(): group_coeffs = lax.psum(up_term, 'narrow')  61 us
    psum x1, waiting for transfers between devices, shards(): group_out = lax.psum(partial_value, 'narrow')  58.3 us
    all_gather x1, waiting for transfers between devices, shards(): all_groups = lax.all_gather(group_coeffs[None], 'wide', axis=0, tiled=True)  45.5 us
    dot_general x1, matrix products, shards(): jnp.einsum('ljpq,ljpv->lqv', near_blocks, sources, precision=HIGH)  27 us
    gather x1, local copies, waits for them, and re-layouts, shards(): sources = extended[local_index]  10 us
    dot_general x1, matrix products, shards(): jnp.einsum('lpk,lpv->lkv', row_basis, cotangent, precision=HIGH)  7.71 us
    all_gather x1, waiting for transfers between devices, shards(): siblings = lax.all_gather(node_coeffs[None], 'narrow', axis=0, tiled=True)  5.84 us
  transfers between devices with their start and end apart: 6, of which 5 were waited for; matrix products, arithmetic and copies ran while one was open for 8% of the time, Pallas kernels for 0%

commit v1 on v0

--- a/solution.py
+++ b/solution.py
@@ -34,7 +34,10 @@
     leaf_coeffs = jnp.einsum("lpk,lpv->lkv", row_basis, cotangent, precision=HIGH)
     node_coeffs = jnp.einsum("lkm,lkv->mv", leaf_up, leaf_coeffs, precision=HIGH)
     up_term = jnp.dot(node_up[0].T, node_coeffs, precision=HIGH)
-    siblings = lax.all_gather(node_coeffs[None], "narrow", axis=0, tiled=True)
+    siblings = jnp.concatenate(
+        lax.all_to_all(jnp.stack([node_coeffs[None]] * lax.axis_size("narrow")), "narrow", 0, 0),
+        axis=0,
+    )
     group_coeffs = lax.psum(up_term, "narrow")
     picked = siblings[far_nodes[0]]
     node_out = jnp.einsum("jkm,jkv->mv", node_couple[0], picked, precision=HIGH)

time: 260 us -> 230 us (0.88)
  waiting for transfers between devices: 173 us -> 139 us
  starting transfers between devices: 2.91 us -> 7.39 us
    all_gather x1, waiting for transfers between devices: 45.5 us -> 15.4 us  [shards(): all_groups = lax.all_gather(group_coeffs[None], 'wide', axis=0, tiled=True)]
    all_gather x1 -> x0, waiting for transfers between devices: 5.84 us -> none  [shards(): siblings = lax.all_gather(node_coeffs[None], 'narrow', axis=0, tiled=True)]
    all_to_all x0 -> x1, starting transfers between devices: none -> 3.56 us  [shards(): lax.all_to_all(jnp.stack([node_coeffs[None]] * lax.axis_size('narrow')),...]
  transfers between devices with their start and end apart: 6 -> 6, of which waited for: 5 -> 4; matrix products, arithmetic and copies ran while one was open for 8% -> 8% of each run, Pallas kernels for 0% -> 0%
where the time goes in v1:
time: 230 us
  waiting for transfers between devices  139 us (60%)
  matrix products  46.2 us (20%)
  local copies, waits for them, and re-layouts  19.3 us (8%)
  between operations  14 us (6%)
  starting transfers between devices  7.39 us (3%)
  other arithmetic  4.46 us (2%)
    psum x1, waiting for transfers between devices, shards(): group_coeffs = lax.psum(up_term, 'narrow')  61.8 us
    psum x1, waiting for transfers between devices, shards(): group_out = lax.psum(partial_value, 'narrow')  58.5 us
    dot_general x1, matrix products, shards(): jnp.einsum('ljpq,ljpv->lqv', near_blocks, sources, precision=HIGH)  27 us
    all_gather x1, waiting for transfers between devices, shards(): all_groups = lax.all_gather(group_coeffs[None], 'wide', axis=0, tiled=True)  15.4 us
    gather x1, local copies, waits for them, and re-layouts, shards(): sources = extended[local_index]  9.91 us
    dot_general x1, matrix products, shards(): jnp.einsum('lpk,lpv->lkv', row_basis, cotangent, precision=HIGH)  7.71 us
  transfers between devices with their start and end apart: 6, of which 4 were waited for; matrix products, arithmetic and copies ran while one was open for 8% of the time, Pallas kernels for 0%

profile of v1, /device:TPU:0, one launch (start us, length us, event | category | flops | bytes accessed | tf_op | source)
XLA Modules:
  0.0 230.0 jit_solution(17238791322925021657)
XLA Ops:
  6.5 7.7 %fusion.14 = f32[12,128,256]{1,2,0:T(8,128)S(1)} fusion(f32[12,256,128]{2,1,0:T(8,128)} %param.14, f32[12,256,256]{2,1,0:T(8,128)} %param.13), kind=kOutput, calls=%fused_computation.26 | convolution fusion | flops 1207959552 | bytes 6291456 | tf_op jit(solution)/shard_map/lpk,lpv->lkv/dot_general | solution.py:34
  14.3 1.4 fusion.15
  15.7 0.9 convolution_bitcast_fusion.2
  16.7 61.8 %all-reduce.3.cloned.1.call-done = f32[1,128,256]{1,2,0:T(8,128)} async-done(((f32[1,128,256]{1,2,0:T(8,128)}), f32[1,128,256]{1,2,0:T(8,128)}) %all-reduce.3.cloned.1.call-update) | async-done | bytes 131088 | tf_op jit(solution)/shard_map/psum | solution.py:41
  78.5 1.7 copy.41
  80.3 1.1 stack.3
  81.3 3.6 %all-to-all-start = ((f32[8,1,128,256]{3,2,1,0:T(8,128)}), f32[8,1,128,256]{3,2,1,0:T(8,128)S(1)}, u32[]{:S(2)}, u32[]{:S(2)}) async-start(f32[8,1,128,256]{3,2,1,0:T(8,128)} %stack.3), calls=%async_computation | async-start | bytes 2097152 | tf_op jit(solution)/shard_map/all_to_all | solution.py:38
  85.0 2.3 fusion.13
  87.3 2.3 collective-permute-start
  89.5 1.5 collective-permute-start.1
  91.7 0.1 copy.42
  92.0 2.9 %collective-permute-done.1 = f32[2,256,256]{2,1,0:T(8,128)} collective-permute-done((f32[2,256,256]{2,1,0:T(8,128)}, f32[2,256,256]{2,1,0:T(8,128)}, u32[]{:S(2)}, u32[]{:S(2)}) %collective-permute-start.1) | collective-permute-done | bytes 524320 | tf_op jit(solution)/shard_map/ppermute | solution.py:13
  94.8 4.4 %pad_maximum_fusion = f32[16,256,256]{2,1,0:T(8,128)} fusion(f32[2,256,256]{2,1,0:T(8,128)} %collective-permute-done.1, f32[12,256,256]{2,1,0:T(8,128)} %param.13, f32[2,256,256]{2,1,0:T(8,128)S(1)} %collective-permute-done), kind=kLoop, calls=%fused_computation.2 | loop fusion | flops 2097152 | bytes 8388608 | tf_op jit(solution)/shard_map/concatenate | solution.py:51
  99.3 9.9 %gather_fusion.1 = f32[48,256,256]{2,1,0:T(8,128)} fusion(f32[16,256,256]{2,1,0:T(8,128)} %pad_maximum_fusion, s32[1024]{0:T(1024)S(1)} %pad_clamp_fusion), kind=kCustom, calls=%fused_computation.1 | custom fusion | bytes 25166016 | tf_op jit(solution)/shard_map/gather | solution.py:55
  109.2 0.6 gather_fusion
  109.7 15.4 %all-gather.2.cloned.1.call-done = f32[16,128,256]{2,1,0:T(8,128)} async-done(((f32[1,128,256]{2,1,0:T(8,128)}), f32[16,128,256]{2,1,0:T(8,128)}) %all-gather.2.cloned.1.call-update) | async-done | bytes 2097168 | tf_op jit(solution)/shard_map/all_gather | solution.py:44
  125.2 1.9 convolution_bitcast_fusion.1
  127.2 0.6 convolution_bitcast_fusion
  127.8 58.5 %all-reduce.5.cloned.1.call-done = f32[128,256]{0,1:T(8,128)} async-done(((f32[128,256]{0,1:T(8,128)}), f32[128,256]{0,1:T(8,128)}) %all-reduce.5.cloned.1.call-update) | async-done | bytes 131088 | tf_op jit(solution)/shard_map/psum | solution.py:47
  186.2 1.2 fusion.3
  187.4 2.5 %fusion.16 = f32[256,12,128]{2,0,1:T(8,128)S(1)} fusion(f32[256,128,1]{1,0,2:T(8,128)S(1)} %fusion.3, f32[12,128,128]{2,1,0:T(8,128)} %param.21), kind=kOutput, calls=%fused_computation.28 | convolution fusion | flops 603979776 | bytes 2490368 | tf_op jit(solution)/shard_map/lmk,kv->lmv/dot_general | solution.py:49
  190.0 2.9 %fusion.1 = f32[12,256,256]{2,1,0:T(8,128)S(1)} fusion(f32[12,256,128]{2,1,0:T(8,128)S(1)} %copy-done, f32[256,12,128]{2,0,1:T(8,128)S(1)} %fusion.16), kind=kOutput, calls=%fused_computation.5 | convolution fusion | flops 1207959552 | bytes 6291456 | tf_op jit(solution)/shard_map/lpk,lkv->lpv/dot_general | solution.py:50
  192.9 27.0 %fusion = f32[12,256,256]{1,2,0:T(8,128)} fusion(f32[12,256,256]{2,1,0:T(8,128)S(1)} %fusion.1, f32[12,4,256,256]{3,2,1,0:T(8,128)} %bitcast.62, f32[12,4,256,256]{3,2,1,0:T(8,128)} %param.22), kind=kOutput, calls=%fused_computation.4 | convolution fusion | flops 9664462848 | bytes 31457280 | tf_op jit(solution)/shard_map/ljpq,ljpv->lqv/dot_general | solution.py:56
  219.9 3.5 %copy.44 = f32[12,256,256]{2,1,0:T(8,128)} copy(f32[12,256,256]{1,2,0:T(8,128)} %fusion) | data formatting | bytes 6291456 | tf_op jit(solution)/shard_map/add | solution.py:57
  (30 shorter events, 0.4 us)
Async XLA Ops:
  6.5 183.4 %copy-start = (f32[12,256,128]{2,1,0:T(8,128)S(1)}, f32[12,256,128]{2,1,0:T(8,128)}, u32[]{:S(2)}) copy-start(f32[12,256,128]{2,1,0:T(8,128)} %param.15) | copy-start | bytes 4718596
  6.5 7.7 %copy-start.1 = (f32[12,128,128]{2,1,0:T(8,128)S(1)}, f32[12,128,128]{2,1,0:T(8,128)}, u32[]{:S(2)}) copy-start(f32[12,128,128]{2,1,0:T(8,128)} %param.16) | copy-start | bytes 2359300
  6.5 9.1 %copy-start.3 = (f32[1,128,128]{2,1,0:T(8,128)S(1)}, f32[1,128,128]{2,1,0:T(8,128)}, u32[]{:S(2)}) copy-start(f32[1,128,128]{2,1,0:T(8,128)} %param.17) | copy-start | bytes 196612
  6.5 72.0 %all-reduce.3.cloned.1.call-start = ((), (), s32[]{:S(2)}) async-start(), calls=%async_computation.1 | async-start | bytes 262144 | tf_op jit(solution)/shard_map/psum | solution.py:41
  16.6 74.4 %copy-start.6 = (s32[12,4]{0,1:T(4,128)S(1)}, s32[12,4]{0,1:T(4,128)}, u32[]{:S(2)}) copy-start(s32[12,4]{0,1:T(4,128)} %param.23) | copy-start | bytes 580
  16.6 75.3 %copy-start.7 = (s32[1,2]{1,0:T(1,128)S(1)}, s32[1,2]{1,0:T(1,128)}, u32[]{:S(2)}) copy-start(s32[1,2]{1,0:T(1,128)} %param.24) | copy-start | bytes 28
  16.6 108.6 %all-gather.2.cloned.1.call-start = ((), (), s32[]{:S(2)}) async-start(), calls=%async_computation.2 | async-start | bytes 2228224 | tf_op jit(solution)/shard_map/all_gather | solution.py:44
  81.3 27.8 %all-to-all-start = ((f32[8,1,128,256]{3,2,1,0:T(8,128)}), f32[8,1,128,256]{3,2,1,0:T(8,128)S(1)}, u32[]{:S(2)}, u32[]{:S(2)}) async-start(f32[8,1,128,256]{3,2,1,0:T(8,128)} %stack.3), calls=%async_computation | async-start | bytes 2097152 | tf_op jit(solution)/shard_map/all_to_all | solution.py:38
  84.9 101.3 %all-reduce.5.cloned.1.call-start = ((), (), s32[]{:S(2)}) async-start(), calls=%async_computation.3 | async-start | bytes 262144 | tf_op jit(solution)/shard_map/psum | solution.py:47
  87.3 4.7 %collective-permute-start = (f32[2,256,256]{2,1,0:T(8,128)}, f32[2,256,256]{2,1,0:T(8,128)S(1)}, u32[]{:S(2)}, u32[]{:S(2)}) collective-permute-start(f32[2,256,256]{2,1,0:T(8,128)} %get-tuple-element.16), channel_id=1, source_target_pairs={{0,1},{1,2},{2,3},{3,4},{4,5},{5,6},{6,7},{7,8},{8,9},{9,10},{10,1... | collective-permute-start | bytes 1572872 | tf_op jit(solution)/shard_map/ppermute | solution.py:13
  89.5 5.3 %collective-permute-start.1 = (f32[2,256,256]{2,1,0:T(8,128)}, f32[2,256,256]{2,1,0:T(8,128)}, u32[]{:S(2)}, u32[]{:S(2)}) collective-permute-start(f32[2,256,256]{2,1,0:T(8,128)} %get-tuple-element.17), channel_id=1, source_target_pairs={{1,0},{2,1},{3,2},{4,3},{5,4},{6,5},{7,6},{8,7},{9,8},{10,9},{11,1... | collective-permute-start | bytes 1572872 | tf_op jit(solution)/shard_map/ppermute | solution.py:13
  99.2 25.9 %copy-start.4 = (f32[1,1,128,128]{3,2,1,0:T(8,128)S(1)}, f32[1,1,128,128]{3,2,1,0:T(8,128)}, u32[]{:S(2)}) copy-start(f32[1,1,128,128]{3,2,1,0:T(8,128)} %param.19) | copy-start | bytes 196612
  99.2 27.9 %copy-start.2 = (f32[1,2,128,128]{3,2,1,0:T(8,128)S(1)}, f32[1,2,128,128]{3,2,1,0:T(8,128)}, u32[]{:S(2)}) copy-start(f32[1,2,128,128]{3,2,1,0:T(8,128)} %param.18) | copy-start | bytes 393220
  99.2 87.0 %copy-start.5 = (f32[1,128,128]{2,1,0:T(8,128)S(1)}, f32[1,128,128]{2,1,0:T(8,128)}, u32[]{:S(2)}) copy-start(f32[1,128,128]{2,1,0:T(8,128)} %param.20) | copy-start | bytes 196612
Sparse Core Ops, SparseCore 0:
  16.8 61.6 all-reduce.2
  80.9 44.2 all-gather.1
  127.6 58.5 all-reduce.4
